TPU v7x, 32 devices: a whole 2x2x4 slice. The times are simulated.
32 devices in a mesh: track: 16 (over z, x, core), ses: 2 (over y).
Axes of the slice: x: 2, y: 2, z: 4, core: 2. Of those that a mesh axis runs over, the one named last changes fastest.
Arguments:
- jacobians: float32 [2, 9, 8, 8192], P(None, None, None, ('track', 'ses')), may hold values from -6 to 6
- direction: float32 [6, 131072], P(None, ('track', 'ses')), may hold values from -50 to 50
- residual: float32 [6, 131072], P(None, ('track', 'ses')), may hold values from -50 to 50
- solution: float32 [6, 131072], P(None, ('track', 'ses')), may hold values from -6 to 6
- cam_damping: float32 [6, 131072], P(None, ('track', 'ses')), may hold values from 0.5 to 4
- precond: float32 [6, 6, 131072], P(None, None, ('track', 'ses')), may hold values from -0.15 to 2, as said below
- land_damping: float32 [8192], P(('track', 'ses')), may hold values from 0.5 to 4
- obs_slot: int32 [8, 8192], P(None, ('track', 'ses')), may hold values from 0 to 511, as said below
- obs_mask: int32 [8, 8192], P(None, ('track', 'ses')), may hold values from 0 to 1, as said below
- serve_rows: int32 [32, 512], P(('track', 'ses')), may hold values from 0 to 4095, as said below
Outputs:
- solution_new: float32 [6, 131072], P(None, ('track', 'ses'))
- residual_new: float32 [6, 131072], P(None, ('track', 'ses'))
- direction_new: float32 [6, 131072], P(None, ('track', 'ses'))
Inputs may be any that keep to these rules, and one draw needn't show every extreme that they name: `obs_slot`: each slot names one keyframe that device s // 16 serves to the observing device; most slots name an owner in the observing device's own session block, the rest name owners anywhere. `serve_rows`: each row block of 16 entries lists distinct local keyframe rows of the owner. `obs_mask`: A track's live observation slots come first; every track has 2 to 8. `precond`: Symmetric, with a dominant positive diagonal.
All inputs are finite; a program needn't handle non-finite values.
Results may differ from a plain program's by a relative error of at most 0.0003.
Values sent between devices are 32-bit elements; how exact they have to be, the bound alone decides.
No kernel may reach another device: no remote copies, remote signals or barrier semaphores. Data moves between devices by JAX's collectives and lax.ppermute only.
A program may use at most 64 MiB of HBM per device.

v0:
```python
import jax
import jax.numpy as jnp
from jax import lax
from jax.sharding import PartitionSpec as P


def invert_three(matrix):
    cofactor = [
        [
            matrix[(i + 1) % 3, (j + 1) % 3] * matrix[(i + 2) % 3, (j + 2) % 3]
            - matrix[(i + 1) % 3, (j + 2) % 3] * matrix[(i + 2) % 3, (j + 1) % 3]
            for j in range(3)
        ]
        for i in range(3)
    ]
    determinant = (
        matrix[0, 0] * cofactor[0][0]
        + matrix[0, 1] * cofactor[0][1]
        + matrix[0, 2] * cofactor[0][2]
    )
    adjugate = jnp.stack([jnp.stack([cofactor[j][i] for j in range(3)]) for i in range(3)])
    return adjugate / determinant[None, None]


def track_terms(jacobian, camera_rows, live_mask, land_damp):
    cam_jac = jacobian[:, 0:6]
    land_jac = jacobian[:, 6:9]
    projected = jnp.sum(cam_jac * camera_rows[None], axis=1)
    weighted = land_jac * live_mask[None, None]
    normal_mat = jnp.sum(weighted[:, :, None] * land_jac[:, None, :], axis=(0, 3))
    identity_mat = (jnp.arange(3)[:, None] == jnp.arange(3)[None, :]).astype(jnp.float32)
    normal_mat = normal_mat + identity_mat[:, :, None] * land_damp[None, None]
    inverse = invert_three(normal_mat)
    landmark_rhs = jnp.sum(weighted * projected[:, None], axis=(0, 2))
    landmark_step = jnp.sum(inverse * landmark_rhs[None], axis=1)
    back_proj = jnp.sum(land_jac * landmark_step[None, :, None], axis=1)
    obs_res = live_mask[None] * (projected - back_proj)
    return jnp.sum(cam_jac * obs_res[:, None], axis=0)


def apply_precond(precond, vector):
    return jnp.sum(precond * vector[None], axis=1)


def on_device(
    jacobians,
    direction,
    residual,
    solution,
    cam_damping,
    precond,
    land_damping,
    obs_slot,
    obs_mask,
    serve_rows,
):
    track_count = lax.axis_size("track")
    ses_count = lax.axis_size("ses")
    served = serve_rows.reshape(-1)
    capacity = served.shape[0] // (track_count * ses_count)
    outgoing = direction[:, served].reshape(6, track_count, ses_count, capacity)
    incoming = lax.all_to_all(
        lax.all_to_all(outgoing, "track", split_axis=1, concat_axis=1, tiled=True),
        "ses",
        split_axis=2,
        concat_axis=2,
        tiled=True,
    )
    incoming = incoming.reshape(6, -1)
    camera_rows = incoming[:, obs_slot]
    live_mask = obs_mask.astype(jnp.float32)
    gradient = track_terms(jacobians, camera_rows, live_mask, land_damping)
    slot_sums = (
        jnp.zeros(incoming.shape, jnp.float32)
        .at[:, obs_slot.reshape(-1)]
        .add(gradient.reshape(6, -1))
    )
    slot_sums = slot_sums.reshape(6, track_count, ses_count, capacity)
    arrived = lax.all_to_all(
        lax.all_to_all(slot_sums, "track", split_axis=1, concat_axis=1, tiled=True),
        "ses",
        split_axis=2,
        concat_axis=2,
        tiled=True,
    )
    summed = jnp.zeros(direction.shape, jnp.float32).at[:, served].add(arrived.reshape(6, -1))
    schur_image = cam_damping * direction + summed
    precond_old = apply_precond(precond, residual)
    old_norm = lax.psum(jnp.sum(residual * precond_old), ("track", "ses"))
    curvature = lax.psum(jnp.sum(direction * schur_image), ("track", "ses"))
    step_size = old_norm / curvature
    solution_new = solution + step_size * direction
    residual_new = residual - step_size * schur_image
    precond_res = apply_precond(precond, residual_new)
    new_norm = lax.psum(jnp.sum(residual_new * precond_res), ("track", "ses"))
    direction_new = precond_res + new_norm / old_norm * direction
    return (solution_new, residual_new, direction_new)


def solution(mesh):
    return jax.shard_map(
        on_device,
        mesh=mesh,
        in_specs=(
            P(None, None, None, ("track", "ses")),
            P(None, ("track", "ses")),
            P(None, ("track", "ses")),
            P(None, ("track", "ses")),
            P(None, ("track", "ses")),
            P(None, None, ("track", "ses")),
            P(("track", "ses")),
            P(None, ("track", "ses")),
            P(None, ("track", "ses")),
            P(("track", "ses"), None),
        ),
        out_specs=(P(None, ("track", "ses")), P(None, ("track", "ses")), P(None, ("track", "ses"))),
        check_vma=False,
    )
```

profile of v0, /device:TPU:0, one launch (start us, length us, event | category | flops | bytes accessed | tf_op | source)
XLA Modules:
  0.0 184.0 jit_solution(6664906381712615767)
XLA Ops:
  0.7 1.6 copy.115
  4.4 7.4 %all-to-all-start = ((f32[16,1,192]{2,1,0:T(1,128)}), f32[16,1,192]{2,1,0:T(1,128)S(1)}, u32[]{:S(2)}, u32[]{:S(2)}) async-start(f32[16,1,192]{2,1,0:T(1,128)} %reshape.516), calls=%async_computation | async-start | bytes 32768 | tf_op jit(solution)/shard_map/all_to_all | solution.py:63
  12.4 5.8 %all-to-all-done = f32[16,1,192]{2,1,0:T(1,128)S(1)} async-done(((f32[16,1,192]{2,1,0:T(1,128)}), f32[16,1,192]{2,1,0:T(1,128)S(1)}, u32[]{:S(2)}, u32[]{:S(2)}) %all-to-all-start) | async-done | bytes 12320 | tf_op jit(solution)/shard_map/all_to_all | solution.py:63
  20.4 3.2 %all-to-all-start.1 = ((f32[2,1,1536]{2,1,0:T(1,128)}), f32[2,1,1536]{2,1,0:T(1,128)S(1)}, u32[]{:S(2)}, u32[]{:S(2)}) async-start(f32[2,1,1536]{2,1,0:T(1,128)} %reshape.518), calls=%async_computation.1 | async-start | bytes 24576 | tf_op jit(solution)/shard_map/all_to_all | solution.py:62
  24.2 3.2 %all-to-all-done.1 = f32[2,1,1536]{2,1,0:T(1,128)S(1)} async-done(((f32[2,1,1536]{2,1,0:T(1,128)}), f32[2,1,1536]{2,1,0:T(1,128)S(1)}, u32[]{:S(2)}, u32[]{:S(2)}) %all-to-all-start.1) | async-done | bytes 12320 | tf_op jit(solution)/shard_map/all_to_all | solution.py:62
  28.6 7.6 %gather_fusion.1 = f32[2048,6]{1,0:T(8,128)} fusion(f32[6,512]{0,1:T(8,128)S(1)} %bitcast.57, s32[2048]{0:T(1024)S(1)} %broadcast_clamp_fusion), kind=kCustom, calls=%fused_computation.1 | custom fusion | bytes 106496 | tf_op jit(solution)/shard_map/gather | solution.py:70
  36.2 1.5 copy.108
  40.9 11.9 %scatter_custom_fusion = f32[6,512]{0,1:T(8,128)S(1)} fusion(s32[2048]{0:T(1024)} %bitcast.76, f32[2048,6]{1,0:T(8,128)} %bitcast.59, f32[]{:T(128)} %constant.4.clone.1), kind=kCustom, calls=%fused_computation.11 | custom fusion | flops 12288 | bytes 12800 | tf_op jit(solution)/shard_map/scatter-add | solution.py:76
  53.8 3.5 %all-to-all-start.2 = ((f32[16,1,192]{2,1,0:T(1,128)}), f32[16,1,192]{2,1,0:T(1,128)S(1)}, u32[]{:S(2)}, u32[]{:S(2)}) async-start(f32[16,1,192]{2,1,0:T(1,128)} %reshape.520), calls=%async_computation.2 | async-start | bytes 32768 | tf_op jit(solution)/shard_map/all_to_all | solution.py:80
  57.6 6.2 %all-to-all-done.2 = f32[16,1,192]{2,1,0:T(1,128)S(1)} async-done(((f32[16,1,192]{2,1,0:T(1,128)}), f32[16,1,192]{2,1,0:T(1,128)S(1)}, u32[]{:S(2)}, u32[]{:S(2)}) %all-to-all-start.2) | async-done | bytes 12320 | tf_op jit(solution)/shard_map/all_to_all | solution.py:80
  65.3 3.2 %all-to-all-start.3 = ((f32[2,1,1536]{2,1,0:T(1,128)}), f32[2,1,1536]{2,1,0:T(1,128)S(1)}, u32[]{:S(2)}, u32[]{:S(2)}) async-start(f32[2,1,1536]{2,1,0:T(1,128)} %reshape.522), calls=%async_computation.3 | async-start | bytes 24576 | tf_op jit(solution)/shard_map/all_to_all | solution.py:79
  69.9 2.5 %all-to-all-done.3 = f32[2,1,1536]{2,1,0:T(1,128)S(1)} async-done(((f32[2,1,1536]{2,1,0:T(1,128)}), f32[2,1,1536]{2,1,0:T(1,128)S(1)}, u32[]{:S(2)}, u32[]{:S(2)}) %all-to-all-start.3) | async-done | bytes 12320 | tf_op jit(solution)/shard_map/all_to_all | solution.py:79
  73.6 4.2 %scatter_fusion = f32[6,4096]{0,1:T(8,128)S(1)} fusion(f32[6,4096]{0,1:T(8,128)S(1)} %copy.113, s32[512]{0:T(512)} %bitcast.75, f32[512,6]{1,0:T(8,128)S(1)} %copy.114), kind=kCustom, calls=%fused_computation.3 | custom fusion | flops 3072 | bytes 38912 | tf_op jit(solution)/shard_map/scatter-add | solution.py:86
  77.8 2.7 %multiply_reduce_fusion.1 = f32[]{:T(128)} fusion(f32[6,4096]{0,1:T(8,128)} %copy-done.1, f32[6,4096]{0,1:T(8,128)S(1)} %scatter_fusion), kind=kLoop, calls=%fused_computation.6 | loop fusion | flops 49151 | bytes 196612 | tf_op jit(solution)/shard_map/reduce_sum | solution.py:90
  80.6 1.9 %copy.119 = f32[6,4096]{0,1:T(8,128)} copy(f32[6,4096]{1,0:T(8,128)S(1)} %copy-done.4) | data formatting | bytes 196608 | tf_op args[2]
  82.5 38.6 %all-reduce = (f32[]{:T(128)}, f32[]{:T(128)}) all-reduce(f32[]{:T(128)} %multiply_reduce_fusion.5, f32[]{:T(128)} %multiply_reduce_fusion.1), channel_id=1, replica_groups=mesh['track'=16,'ses'=2] {'track','ses'}, use_global_device_ids=true, to_apply=%region_2.0 | all-reduce | flops 2 | bytes 16 | tf_op jit(solution)/shard_map/psum | solution.py:89
  122.4 3.1 %multiply_subtract_fusion = f32[6,4096]{0,1:T(8,128)} fusion(f32[6,4096]{0,1:T(8,128)} %copy.119, f32[6,4096]{0,1:T(8,128)S(1)} %scatter_fusion, f32[]{:T(128)S(6)} %div.19), kind=kLoop, calls=%fused_computation.5 | loop fusion | flops 49152 | bytes 294916 | tf_op jit(solution)/shard_map/sub | solution.py:93
  125.5 2.2 %copy.123 = f32[6,4096]{1,0:T(8,128)S(1)} copy(f32[6,4096]{0,1:T(8,128)} %multiply_subtract_fusion) | data formatting | bytes 196608
  128.0 2.0 %copy.121 = f32[6,4096]{0,1:T(8,128)} copy(f32[6,4096]{1,0:T(8,128)S(1)} %multiply_reduce_fusion.2) | data formatting | bytes 196608 | tf_op jit(solution)/shard_map/reduce_sum | solution.py:42
  130.0 2.8 %multiply_reduce_fusion = f32[]{:T(128)} fusion(f32[6,4096]{0,1:T(8,128)S(1)} %copy-done, f32[6,4096]{0,1:T(8,128)} %copy.121), kind=kLoop, calls=%fused_computation.4 | loop fusion | flops 49151 | bytes 196612 | tf_op jit(solution)/shard_map/reduce_sum | solution.py:95
  133.4 40.5 %psum.23 = f32[]{:T(128)} all-reduce(f32[]{:T(128)} %multiply_reduce_fusion), channel_id=1, replica_groups=mesh['track'=16,'ses'=2] {'track','ses'}, use_global_device_ids=true, to_apply=%region_15.0 | all-reduce | flops 1 | bytes 8 | tf_op jit(solution)/shard_map/psum | solution.py:95
  176.0 2.0 %copy.118 = f32[6,4096]{0,1:T(8,128)} copy(f32[6,4096]{1,0:T(8,128)S(1)} %get-tuple-element.31) | data formatting | bytes 196608 | tf_op jit(solution)/shard_map/mul | solution.py:92
  177.9 3.2 %add.67 = f32[6,4096]{0,1:T(8,128)} add(f32[6,4096]{0,1:T(8,128)S(1)} %copy.117, f32[6,4096]{0,1:T(8,128)} %copy.118) | non-fusion elementwise | flops 24576 | bytes 294912 | tf_op jit(solution)/shard_map/add | solution.py:92
  181.1 2.9 %copy.122 = f32[6,4096]{1,0:T(8,128)} copy(f32[6,4096]{0,1:T(8,128)} %add.67) | data formatting | bytes 196608
  (79 shorter events, 16.6 us)
Async XLA Ops:
  0.6 1.6 copy-start.13
  0.6 11.1 %copy-start.10 = (s32[8,256]{1,0:T(8,128)S(1)}, s32[8,256]{1,0:T(8,128)}, u32[]{:S(2)}) copy-start(s32[8,256]{1,0:T(8,128)} %param.17) | copy-start | bytes 24580
  0.7 23.6 %copy-start.12 = (s32[8,256]{1,0:T(8,128)S(1)}, s32[8,256]{1,0:T(8,128)}, u32[]{:S(2)}) copy-start(s32[8,256]{1,0:T(8,128)} %param.18) | copy-start | bytes 24580
  2.2 38.6 %copy-start.1 = (f32[6,4096]{0,1:T(8,128)}, f32[6,4096]{0,1:T(8,128)S(1)}, u32[]{:S(2)}) copy-start(f32[6,4096]{0,1:T(8,128)S(1)} %copy.115) | copy-start | bytes 294916
  2.2 35.5 %copy-start.5 = (f32[2,9,8,256]{3,2,1,0:T(8,128)S(1)}, f32[2,9,8,256]{3,2,1,0:T(8,128)}, u32[]{:S(2)}) copy-start(f32[2,9,8,256]{3,2,1,0:T(8,128)} %param.10) | copy-start | bytes 442372
  2.3 1.1 copy-start.11
  4.4 13.9 %all-to-all-start = ((f32[16,1,192]{2,1,0:T(1,128)}), f32[16,1,192]{2,1,0:T(1,128)S(1)}, u32[]{:S(2)}, u32[]{:S(2)}) async-start(f32[16,1,192]{2,1,0:T(1,128)} %reshape.516), calls=%async_computation | async-start | bytes 32768 | tf_op jit(solution)/shard_map/all_to_all | solution.py:63
  20.4 7.1 %all-to-all-start.1 = ((f32[2,1,1536]{2,1,0:T(1,128)}), f32[2,1,1536]{2,1,0:T(1,128)S(1)}, u32[]{:S(2)}, u32[]{:S(2)}) async-start(f32[2,1,1536]{2,1,0:T(1,128)} %reshape.518), calls=%async_computation.1 | async-start | bytes 24576 | tf_op jit(solution)/shard_map/all_to_all | solution.py:62
  24.2 13.5 %copy-start.9 = (f32[8,256]{1,0:T(8,128)}, f32[8,256]{1,0:T(8,128)S(1)}, u32[]{:S(2)}) copy-start(f32[8,256]{1,0:T(8,128)S(1)} %convert_element_type.10) | copy-start | bytes 24580
  28.6 28.7 %copy-start.2 = (f32[6,6,4096]{2,1,0:T(8,128)S(1)}, f32[6,6,4096]{2,1,0:T(8,128)}, u32[]{:S(2)}) copy-start(f32[6,6,4096]{2,1,0:T(8,128)} %param.15) | copy-start | bytes 1769476
  28.6 28.7 %copy-start.4 = (f32[6,4096]{1,0:T(8,128)S(1)}, f32[6,4096]{1,0:T(8,128)}, u32[]{:S(2)}) copy-start(f32[6,4096]{1,0:T(8,128)} %param.12) | copy-start | bytes 294916
  37.8 31.4 %copy-start.3 = (f32[6,4096]{1,0:T(8,128)S(1)}, f32[6,4096]{1,0:T(8,128)}, u32[]{:S(2)}) copy-start(f32[6,4096]{1,0:T(8,128)} %param.11) | copy-start | bytes 294916
  37.8 31.4 %copy-start.7 = (f32[6,4096]{1,0:T(8,128)S(1)}, f32[6,4096]{1,0:T(8,128)}, u32[]{:S(2)}) copy-start(f32[6,4096]{1,0:T(8,128)} %param.14) | copy-start | bytes 294916
  53.8 10.0 %all-to-all-start.2 = ((f32[16,1,192]{2,1,0:T(1,128)}), f32[16,1,192]{2,1,0:T(1,128)S(1)}, u32[]{:S(2)}, u32[]{:S(2)}) async-start(f32[16,1,192]{2,1,0:T(1,128)} %reshape.520), calls=%async_computation.2 | async-start | bytes 32768 | tf_op jit(solution)/shard_map/all_to_all | solution.py:80
  65.3 7.1 %all-to-all-start.3 = ((f32[2,1,1536]{2,1,0:T(1,128)}), f32[2,1,1536]{2,1,0:T(1,128)S(1)}, u32[]{:S(2)}, u32[]{:S(2)}) async-start(f32[2,1,1536]{2,1,0:T(1,128)} %reshape.522), calls=%async_computation.3 | async-start | bytes 24576 | tf_op jit(solution)/shard_map/all_to_all | solution.py:79
  127.7 5.0 %copy-start.6 = (f32[6,4096]{1,0:T(8,128)}, f32[6,4096]{1,0:T(8,128)S(1)}, u32[]{:S(2)}) copy-start(f32[6,4096]{1,0:T(8,128)S(1)} %copy.123) | copy-start | bytes 294916
  127.7 2.3 %copy-start = (f32[6,4096]{0,1:T(8,128)S(1)}, f32[6,4096]{0,1:T(8,128)}, u32[]{:S(2)}) copy-start(f32[6,4096]{0,1:T(8,128)} %multiply_subtract_fusion) | copy-start | bytes 294916
  130.0 2.8 %copy-start.8 = (f32[6,4096]{1,0:T(8,128)S(1)}, f32[6,4096]{1,0:T(8,128)}, u32[]{:S(2)}) copy-start(f32[6,4096]{1,0:T(8,128)} %param.13) | copy-start | bytes 294916
where the time goes:
time: 185 us; the launch traced here: 184 us
  blocking collectives  79.1 us (43%)
  other arithmetic  35.5 us (19%)
  local copies, waits for them, and re-layouts  30.6 us (17%)
  waiting for transfers between devices  17.8 us (10%)
  starting transfers between devices  17.3 us (9%)
  between operations  3.72 us (2%)
    psum x1, blocking collectives, on_device(): new_norm = lax.psum(jnp.sum(residual_new * precond_res), ('track', 'ses'))  40.5 us
    psum x1, blocking collectives, on_device(): old_norm = lax.psum(jnp.sum(residual * precond_old), ('track', 'ses'))  38.6 us
    unnamed x43, local copies, waits for them, and re-layouts  12.7 us
    scatter-add x1, other arithmetic, on_device(): slot_sums = jnp.zeros(incoming.shape, jnp.float32).at[:, obs_slot.reshape...  11.9 us
    gather x2, local copies, waits for them, and re-layouts, on_device(): camera_rows = incoming[:, obs_slot]  9.11 us
    all_to_all x1, starting transfers between devices, on_device(): lax.all_to_all(outgoing, 'track', split_axis=1, concat_axis=1, tiled=True)  7.36 us
    all_to_all x1, waiting for transfers between devices, on_device(): lax.all_to_all(slot_sums, 'track', split_axis=1, concat_axis=1, tiled=True)  6.18 us
    all_to_all x1, waiting for transfers between devices, on_device(): lax.all_to_all(outgoing, 'track', split_axis=1, concat_axis=1, tiled=True)  5.83 us
  transfers between devices with their start and end apart: 4, of which 4 were waited for; matrix products, arithmetic and copies ran while one was open for 1% of the time, Pallas kernels for 0%

commit v1 on v0

v1 whole, which is shorter than its diff:
```python
import functools

import jax
import jax.numpy as jnp
from jax import lax
from jax.experimental import pallas as pl
from jax.experimental.pallas import tpu as pltpu
from jax.sharding import PartitionSpec as P

LANES = 128
SUBS = 8
AXES = ("track", "ses")


def lane_gather(rows, index):
    return jnp.take_along_axis(rows, index, axis=1, mode="promise_in_bounds")


def spread(row, subs=SUBS):
    return jnp.broadcast_to(row, (subs, row.shape[1]))


def iota(shape, dim):
    return lax.broadcasted_iota(jnp.int32, shape, dim)


def each(count, body):
    if count <= 8:
        for j in range(count):
            body(j)
    else:
        lax.fori_loop(0, count, lambda j, c: (body(j), c)[1], 0)


def at_group(j):
    if isinstance(j, int):
        return pl.ds(j * LANES, LANES)
    return pl.ds(pl.multiple_of(j * LANES, LANES), LANES)


def at_rows(j, size=SUBS):
    if isinstance(j, int):
        return pl.ds(j * size, size)
    return pl.ds(pl.multiple_of(j * size, size), size)


def rows_to_blocks(rows, cap, params):
    per = LANES // cap
    lane = iota((per, LANES), 1)
    index = iota((per, LANES), 0) * cap + lane % cap
    out = jnp.zeros((per, LANES), rows.dtype)
    for k in range(params):
        picked = lane_gather(spread(rows[k : k + 1], per), index)
        out = jnp.where(lane // cap == k, picked, out)
    return out


def blocks_to_rows(blocks, cap, params):
    per = LANES // cap
    lane = iota((SUBS, LANES), 1)
    sub = iota((SUBS, LANES), 0)
    index = jnp.minimum(sub, params - 1) * cap + lane % cap
    out = jnp.zeros((SUBS, LANES), blocks.dtype)
    for src in range(per):
        picked = lane_gather(spread(blocks[src : src + 1]), index)
        out = jnp.where(lane // cap == src, picked, out)
    return jnp.where(sub < params, out, 0.0)


def split_bf16(value, parts):
    pieces = []
    rest = value
    for p in range(parts):
        piece = rest.astype(jnp.bfloat16)
        pieces.append(piece)
        if p + 1 < parts:
            rest = rest - piece.astype(jnp.float32)
    return pieces


def apply_precond(precond, vector):
    params = vector.shape[0]
    total = precond[0] * vector[0:1]
    for k in range(1, params):
        total = total + precond[k] * vector[k : k + 1]
    return total


def serve_kernel(cap, direction, served, outgoing):
    params, count = direction.shape
    groups = served.shape[1] // LANES
    per = LANES // cap

    def body(j):
        row = served[:, at_group(j)]
        low = spread(row % LANES, params)
        high = spread(row // LANES, params)
        rows = jnp.zeros((params, LANES), jnp.float32)
        for h in range(count // LANES):
            picked = lane_gather(direction[:, h * LANES : (h + 1) * LANES], low)
            rows = jnp.where(high == h, picked, rows)
        outgoing[at_rows(j, per), :] = rows_to_blocks(rows, cap, params)

    each(groups, body)


def norms_kernel(direction, residual, damping, precond, norms):
    params, count = direction.shape
    old = jnp.zeros((params, LANES), jnp.float32)
    curv = jnp.zeros((params, LANES), jnp.float32)
    for h in range(count // LANES):
        at = slice(h * LANES, (h + 1) * LANES)
        res = residual[:, at]
        pre = apply_precond([precond[k, :, at] for k in range(params)], res)
        old = old + res * pre
        dire = direction[:, at]
        curv = curv + damping[:, at] * dire * dire
    row = iota((SUBS, LANES), 0)
    norms[...] = jnp.where(row == 0, jnp.sum(old), jnp.where(row == 1, jnp.sum(curv), 0.0))


def track_kernel(cap, params, incoming, jac, slots, mask, damp, norms, returned, table):
    devices = incoming.shape[0]
    per = LANES // cap
    groups = devices // per
    obs, tracks = slots.shape

    def fill(j):
        table[:, at_group(j)] = blocks_to_rows(incoming[at_rows(j, per), :], cap, params)

    each(groups, fill)

    slot = slots[...]
    owner = slot // cap
    within = slot % cap
    halves = [slice(t * LANES, (t + 1) * LANES) for t in range(tracks // LANES)]
    low = [slot[:, at] % LANES for at in halves]
    high = [slot[:, at] // LANES for at in halves]

    def look(j, camera):
        rows = table[:, at_group(j)]
        out = []
        for k in range(params):
            source = spread(rows[k : k + 1], obs)
            for t in range(len(halves)):
                picked = lane_gather(source, low[t])
                out.append(jnp.where(high[t] == j, picked, camera[len(out)]))
        return tuple(out)

    camera = tuple(jnp.zeros((obs, LANES), jnp.float32) for _ in range(params * len(halves)))
    if groups <= 8:
        for j in range(groups):
            camera = look(j, camera)
    else:
        camera = lax.fori_loop(0, groups, look, camera)
    camera = [
        jnp.concatenate(camera[k * len(halves) : (k + 1) * len(halves)], axis=1)
        for k in range(params)
    ]

    live = mask[...].astype(jnp.float32)
    cam = [[jac[a, k] for k in range(params)] for a in range(2)]
    land = [[jac[a, params + i] for i in range(3)] for a in range(2)]
    projected = []
    for a in range(2):
        total = cam[a][0] * camera[0]
        for k in range(1, params):
            total = total + cam[a][k] * camera[k]
        projected.append(total)
    weighted = [[land[a][i] * live for i in range(3)] for a in range(2)]

    def over_slots(value):
        return jnp.sum(value, axis=0, keepdims=True)

    normal = {}
    for i in range(3):
        for j in range(i, 3):
            entry = over_slots(weighted[0][i] * land[0][j] + weighted[1][i] * land[1][j])
            if i == j:
                entry = entry + damp[...]
            normal[i, j] = entry
            normal[j, i] = entry
    rhs = [over_slots(weighted[0][i] * projected[0] + weighted[1][i] * projected[1]) for i in range(3)]
    cof = [
        [
            normal[(i + 1) % 3, (j + 1) % 3] * normal[(i + 2) % 3, (j + 2) % 3]
            - normal[(i + 1) % 3, (j + 2) % 3] * normal[(i + 2) % 3, (j + 1) % 3]
            for j in range(3)
        ]
        for i in range(3)
    ]
    det = normal[0, 0] * cof[0][0] + normal[0, 1] * cof[0][1] + normal[0, 2] * cof[0][2]
    step = [
        (cof[0][i] * rhs[0] + cof[1][i] * rhs[1] + cof[2][i] * rhs[2]) / det for i in range(3)
    ]
    res = [
        live
        * (projected[a] - (land[a][0] * step[0] + land[a][1] * step[1] + land[a][2] * step[2]))
        for a in range(2)
    ]
    curv = jnp.sum(res[0] * projected[0] + res[1] * projected[1])
    grad = [cam[0][k] * res[0] + cam[1][k] * res[1] for k in range(params)]

    owner_id = iota((devices, tracks), 0)
    within_id = iota((cap, tracks), 0)
    total = jnp.zeros((devices, LANES), jnp.float32)
    pad = LANES - params * cap
    for o in range(obs):
        at_owner = (spread(owner[o : o + 1], devices) == owner_id).astype(jnp.float32).astype(jnp.bfloat16)
        at_within = spread(within[o : o + 1], cap) == within_id
        values = [jnp.where(at_within, spread(grad[k][o : o + 1], cap), 0.0) for k in range(params)]
        if pad:
            values.append(jnp.zeros((pad, tracks), jnp.float32))
        values = jnp.concatenate(values, axis=0)
        for piece in split_bf16(values, 3):
            total = total + lax.dot_general(
                at_owner, piece, (((1,), (1,)), ((), ())), preferred_element_type=jnp.float32
            )
    lane = iota((devices, LANES), 1)
    old_part = spread(norms[0:1, :], devices)
    curv_part = spread(norms[1:2, :], devices) + curv
    total = jnp.where(lane == params * cap, old_part, total)
    returned[...] = jnp.where(lane == params * cap + 1, curv_part, total)


def owner_kernel(
    cap, arrived, served, direction, residual, solution, damping, precond,
    solution_new, residual_new, pre_new, norm_block, old_norm, summed,
):
    params, count = direction.shape
    devices = arrived.shape[0]
    per = LANES // cap
    groups = devices // per
    highs = count // LANES
    low_id = iota((LANES, LANES), 0)

    def body(j, first):
        rows = blocks_to_rows(arrived[at_rows(j, per), :], cap, params)
        row = served[:, at_group(j)]
        at_low = (spread(row % LANES, LANES) == low_id).astype(jnp.float32).astype(jnp.bfloat16)
        high = spread(row // LANES)
        picked = jnp.concatenate([jnp.where(high == h, rows, 0.0) for h in range(highs)], axis=0)
        total = None
        for piece in split_bf16(picked, 3):
            part = lax.dot_general(
                piece, at_low, (((1,), (1,)), ((), ())), preferred_element_type=jnp.float32
            )
            total = part if total is None else total + part
        summed[...] = total if first else summed[...] + total

    body(0, True)
    if groups <= 8:
        for j in range(1, groups):
            body(j, False)
    else:
        lax.fori_loop(1, groups, lambda j, c: (body(j, False), c)[1], 0)

    totals = jnp.sum(arrived[...], axis=0, keepdims=True)
    old = totals[:, params * cap : params * cap + 1]
    curv = totals[:, params * cap + 1 : params * cap + 2]
    step_size = old / curv
    step = jnp.broadcast_to(step_size, (params, LANES))
    new = jnp.zeros((params, LANES), jnp.float32)
    for h in range(highs):
        at = slice(h * LANES, (h + 1) * LANES)
        dire = direction[:, at]
        image = damping[:, at] * dire + summed[h * SUBS : h * SUBS + params, :]
        solution_new[:, at] = solution[:, at] + step * dire
        res = residual[:, at] - step * image
        residual_new[:, at] = res
        pre = apply_precond([precond[k, :, at] for k in range(params)], res)
        pre_new[:, at] = pre
        new = new + res * pre
    norm_block[...] = jnp.broadcast_to(jnp.sum(new), norm_block.shape)
    old_norm[...] = jnp.broadcast_to(old, old_norm.shape)


def final_kernel(norm_blocks, old_norm, direction, pre_new, direction_new):
    new = jnp.sum(norm_blocks[...], axis=0, keepdims=True)
    ratio = new / old_norm[0:1, :]
    params, count = direction.shape
    ratio = jnp.broadcast_to(ratio, (params, LANES))
    for h in range(count // LANES):
        at = slice(h * LANES, (h + 1) * LANES)
        direction_new[:, at] = pre_new[:, at] + ratio * direction[:, at]


def call(kernel, outs, scratch=(), cost=0):
    shapes = [jax.ShapeDtypeStruct(o, jnp.float32) for o in outs]
    return pl.pallas_call(
        kernel,
        out_shape=shapes[0] if len(shapes) == 1 else shapes,
        scratch_shapes=scratch,
        compiler_params=pltpu.CompilerParams(vmem_limit_bytes=32 * 1024 * 1024),
        cost_estimate=pl.CostEstimate(flops=cost, bytes_accessed=cost, transcendentals=0),
    )


def exchange(blocks):
    return lax.all_to_all(blocks, AXES, split_axis=0, concat_axis=0, tiled=True)


def on_device(
    jacobians,
    direction,
    residual,
    solution,
    cam_damping,
    precond,
    land_damping,
    obs_slot,
    obs_mask,
    serve_rows,
):
    devices = lax.axis_size("track") * lax.axis_size("ses")
    params = direction.shape[0]
    cap = serve_rows.shape[1] // devices
    block = (devices, LANES)

    outgoing = call(functools.partial(serve_kernel, cap), [block], cost=400_000)(direction, serve_rows)
    incoming = exchange(outgoing)
    norms = call(norms_kernel, [(SUBS, LANES)], cost=2_000_000)(direction, residual, cam_damping, precond)
    returned = call(
        functools.partial(track_kernel, cap, params),
        [block],
        scratch=[pltpu.VMEM((SUBS, devices * cap), jnp.float32)],
        cost=2_000_000,
    )(incoming, jacobians, obs_slot, obs_mask, land_damping.reshape(1, -1), norms)
    arrived = exchange(returned)
    solution_new, residual_new, pre_new, norm_block, old_norm = call(
        functools.partial(owner_kernel, cap),
        [direction.shape, direction.shape, direction.shape, block, (SUBS, LANES)],
        scratch=[pltpu.VMEM((direction.shape[1] // LANES * SUBS, LANES), jnp.float32)],
        cost=2_000_000,
    )(arrived, serve_rows, direction, residual, solution, cam_damping, precond)
    norm_blocks = exchange(norm_block)
    direction_new = call(final_kernel, [direction.shape], cost=400_000)(
        norm_blocks, old_norm, direction, pre_new
    )
    return (solution_new, residual_new, direction_new)


def solution(mesh):
    return jax.shard_map(
        on_device,
        mesh=mesh,
        in_specs=(
            P(None, None, None, AXES),
            P(None, AXES),
            P(None, AXES),
            P(None, AXES),
            P(None, AXES),
            P(None, None, AXES),
            P(AXES),
            P(None, AXES),
            P(None, AXES),
            P(AXES, None),
        ),
        out_specs=(P(None, AXES), P(None, AXES), P(None, AXES)),
        check_vma=False,
    )
```

time: 185 us -> 39.3 us (0.21)
  blocking collectives: 79.1 us -> 18.4 us
  other arithmetic: 35.5 us -> 0 us
  local copies, waits for them, and re-layouts: 30.6 us -> 4.56 us
  waiting for transfers between devices: 17.8 us -> 3.9 us
  starting transfers between devices: 17.3 us -> 7.3 us
  Pallas kernels: 0 us -> 3.99 us
  between operations: 3.72 us -> 0.74 us
    psum x2 -> x0, blocking collectives: 79.1 us -> none  [the longest x1 40.5 us: on_device(): new_norm = lax.psum(jnp.sum(residual_new * precond_res), ('track', 'ses'))]
    all_to_all x0 -> x2, blocking collectives: none -> 18.4 us  [exchange(): return lax.all_to_all(blocks, AXES, split_axis=0, concat_axis=0, tiled=True)]
    scatter-add x2 -> x0, other arithmetic: 16.1 us -> none  [the longest x1 11.9 us: on_device(): slot_sums = jnp.zeros(incoming.shape, jnp.float32).at[:, obs_slot.reshape...]
    all_to_all x4 -> x1, waiting for transfers between devices: 17.8 us -> 3.9 us  [exchange(): return lax.all_to_all(blocks, AXES, split_axis=0, concat_axis=0, tiled=True)]
    gather x3 -> x0, local copies, waits for them, and re-layouts: 10.1 us -> none  [the longest x2 9.11 us: on_device(): camera_rows = incoming[:, obs_slot]]
    all_to_all x4 -> x1, starting transfers between devices: 17.3 us -> 7.3 us  [exchange(): return lax.all_to_all(blocks, AXES, split_axis=0, concat_axis=0, tiled=True)]
    unnamed x43 -> x30, local copies, waits for them, and re-layouts: 12.7 us -> 4.56 us
    reduce_sum x11 -> x0, other arithmetic: 6.79 us -> none  [the longest x1 2.77 us: on_device(): new_norm = lax.psum(jnp.sum(residual_new * precond_res), ('track', 'ses'))]
  transfers between devices with their start and end apart: 4 -> 1, of which waited for: 4 -> 1; matrix products, arithmetic and copies ran while one was open for 1% -> 0% of each run, Pallas kernels for 0% -> 1%
where the time goes in v1:
time: 39.3 us; the launch traced here: 38.9 us
  blocking collectives  18.4 us (47%)
  starting transfers between devices  7.3 us (19%)
  local copies, waits for them, and re-layouts  4.56 us (12%)
  Pallas kernels  3.99 us (10%)
  waiting for transfers between devices  3.9 us (10%)
  between operations  0.74 us (2%)
    all_to_all x2, blocking collectives, exchange(): return lax.all_to_all(blocks, AXES, split_axis=0, concat_axis=0, tiled=True)  18.4 us
    all_to_all x1, starting transfers between devices, exchange(): return lax.all_to_all(blocks, AXES, split_axis=0, concat_axis=0, tiled=True)  7.3 us
    unnamed x30, local copies, waits for them, and re-layouts  4.56 us
    all_to_all x1, waiting for transfers between devices, exchange(): return lax.all_to_all(blocks, AXES, split_axis=0, concat_axis=0, tiled=True)  3.9 us
    pallas_call x1, Pallas kernels, on_device(): call(functools.partial(owner_kernel, cap), [direction.shape, direction.sh...  1.21 us
    pallas_call x1, Pallas kernels, on_device(): call(functools.partial(serve_kernel, cap), [block], cost=400000)  1.03 us
    pallas_call x1, Pallas kernels, on_device(): call(functools.partial(track_kernel, cap, params), [block], scratch=[pltp...  0.83 us
  transfers between devices with their start and end apart: 1, of which 1 were waited for; matrix products, arithmetic and copies ran while one was open for 0% of the time, Pallas kernels for 1%

profile of v1, /device:TPU:0, one launch (start us, length us, event | category | flops | bytes accessed | tf_op | source)
XLA Modules:
  0.0 38.9 jit_solution(2687027604274692720)
XLA Ops:
  0.6 0.0 copy-start.2
  0.6 0.9 %copy-done.2 = f32[6,4096]{1,0:T(8,128)S(1)} copy-done((f32[6,4096]{1,0:T(8,128)S(1)}, f32[6,4096]{1,0:T(8,128)}, u32[]{:S(2)}) %copy-start.2) | copy-done | bytes 98328
  1.5 0.7 %copy-done.10 = s32[1,512]{1,0:T(1,128)S(1)} copy-done((s32[1,512]{1,0:T(1,128)S(1)}, s32[1,512]{1,0:T(1,128)}, u32[]{:S(2)}) %copy-start.10) | copy-done | bytes 2072
  2.2 1.0 %shard_map.121 = f32[32,128]{1,0:T(8,128)} custom-call(f32[6,4096]{1,0:T(8,128)S(1)} %copy-done.2, s32[1,512]{1,0:T(1,128)S(1)} %copy-done.10), custom_call_target="tpu_custom_call" | custom-call | flops 400000 | bytes 400000 | tf_op jit(solution)/shard_map/pallas_call | solution.py:320
  3.3 7.3 %all-to-all-start = ((f32[32,1,128]{2,1,0:T(1,128)}), f32[32,1,128]{2,1,0:T(1,128)S(1)}, u32[]{:S(2)}, u32[]{:S(2)}) async-start(f32[32,1,128]{2,1,0:T(1,128)} %bitcast.1), calls=%async_computation | async-start | bytes 32768 | tf_op jit(solution)/shard_map/all_to_all | solution.py:300
  10.6 0.0 copy-done.3
  10.6 0.0 copy-start
  10.6 1.1 %copy-done = f32[6,6,4096]{2,1,0:T(8,128)S(1)} copy-done((f32[6,6,4096]{2,1,0:T(8,128)S(1)}, f32[6,6,4096]{2,1,0:T(8,128)}, u32[]{:S(2)}) %copy-start) | copy-done | bytes 589848
  11.7 0.9 %copy-done.4 = f32[6,4096]{1,0:T(8,128)S(1)} copy-done((f32[6,4096]{1,0:T(8,128)S(1)}, f32[6,4096]{1,0:T(8,128)}, u32[]{:S(2)}) %copy-start.4) | copy-done | bytes 98328
  12.6 0.9 %copy-done.6 = f32[6,4096]{1,0:T(8,128)S(1)} copy-done((f32[6,4096]{1,0:T(8,128)S(1)}, f32[6,4096]{1,0:T(8,128)}, u32[]{:S(2)}) %copy-start.6) | copy-done | bytes 98328
  13.5 0.2 shard_map.122.norms
  13.8 0.0 copy-start.5
  13.8 3.9 %all-to-all-done = f32[32,1,128]{2,1,0:T(1,128)S(1)} async-done(((f32[32,1,128]{2,1,0:T(1,128)}), f32[32,1,128]{2,1,0:T(1,128)S(1)}, u32[]{:S(2)}, u32[]{:S(2)}) %all-to-all-start) | async-done | bytes 16416 | tf_op jit(solution)/shard_map/all_to_all | solution.py:300
  17.7 0.0 copy-done.12
  17.7 0.0 copy-done.13
  17.7 0.0 copy-done.14
  17.7 0.0 copy-done.8
  17.7 0.8 %shard_map.123 = f32[32,128]{1,0:T(8,128)S(1)} custom-call(f32[32,128]{1,0:T(8,128)S(1)} %bitcast.13, f32[2,9,8,256]{3,2,1,0:T(8,128)S(1)} %copy-done.8, s32[8,256]{1,0:T(8,128)S(1)} %copy-done.12, s32[8,256]{1,0:T(8,128)S(1)} %copy-done.13, f32[1,256]{1,0:T(1,128)S(1)} %bitcast.18, f32[8,128]{1,0:T(8,128)S(1)} %shard_map.122.norms), custom_call_target="tpu_custom_call" | custom-call | flops 2000000 | bytes 2000000 | tf_op jit(solution)/shard_map/pallas_call | solution.py:323
  18.5 0.0 copy-start.11
  18.6 9.6 %all_to_all.33 = f32[32,1,128]{2,1,0:T(1,128)S(1)} all-to-all(f32[32,1,128]{2,1,0:T(1,128)S(1)} %bitcast.15), channel_id=1, replica_groups=mesh['track'=16,'ses'=2] {'track','ses'}, dimensions={0} | all-to-all | bytes 32768 | tf_op jit(solution)/shard_map/all_to_all | solution.py:300
  28.1 0.0 copy-done.9
  28.2 1.2 %shard_map.124 = (f32[6,4096]{1,0:T(8,128)}, f32[6,4096]{1,0:T(8,128)}, f32[6,4096]{1,0:T(8,128)S(1)}, f32[32,128]{1,0:T(8,128)S(1)}, f32[8,128]{1,0:T(8,128)S(1)}) custom-call(f32[32,128]{1,0:T(8,128)S(1)} %bitcast.16, s32[1,512]{1,0:T(1,128)S(1)} %copy-done.11, f32[6,4096]{1,0:T(8,128)S(1)} %copy-done.3, f32[6,4096]{1,0:T(8,128)S(1)} %copy-done.5, ...), custom_call_target="tpu_custom_call" | custom-call | flops 2000000 | bytes 2000000 | tf_op jit(solution)/shard_map/pallas_call | solution.py:330
  29.4 8.9 %all_to_all.34 = f32[32,1,128]{2,1,0:T(1,128)S(1)} all-to-all(f32[32,1,128]{2,1,0:T(1,128)S(1)} %bitcast.17), channel_id=1, replica_groups=mesh['track'=16,'ses'=2] {'track','ses'}, dimensions={0} | all-to-all | bytes 32768 | tf_op jit(solution)/shard_map/all_to_all | solution.py:300
  38.2 0.7 %shard_map.125 = f32[6,4096]{1,0:T(8,128)} custom-call(f32[32,128]{1,0:T(8,128)S(1)} %bitcast.14, f32[8,128]{1,0:T(8,128)S(1)} %get-tuple-element.11.old_norm, f32[6,4096]{1,0:T(8,128)S(1)} %copy-done.3, f32[6,4096]{1,0:T(8,128)S(1)} %get-tuple-element.12.pre_new), custom_call_target="tpu_custom_call" | custom-call | flops 400000 | bytes 400000 | tf_op jit(solution)/shard_map/pallas_call | solution.py:337
  (15 shorter events, 0.0 us)
Async XLA Ops:
  0.6 0.9 %copy-start.2 = (f32[6,4096]{1,0:T(8,128)S(1)}, f32[6,4096]{1,0:T(8,128)}, u32[]{:S(2)}) copy-start(f32[6,4096]{1,0:T(8,128)} %direction.7) | copy-start | bytes 294916
  1.5 0.7 %copy-start.10 = (s32[1,512]{1,0:T(1,128)S(1)}, s32[1,512]{1,0:T(1,128)}, u32[]{:S(2)}) copy-start(s32[1,512]{1,0:T(1,128)} %served.3) | copy-start | bytes 6148
  2.2 8.3 %copy-start.3 = (f32[6,4096]{1,0:T(8,128)S(1)}, f32[6,4096]{1,0:T(8,128)}, u32[]{:S(2)}) copy-start(f32[6,4096]{1,0:T(8,128)} %direction.7) | copy-start | bytes 294916
  3.3 14.4 %copy-start.12 = (s32[8,256]{1,0:T(8,128)S(1)}, s32[8,256]{1,0:T(8,128)}, u32[]{:S(2)}) copy-start(s32[8,256]{1,0:T(8,128)} %slots.1) | copy-start | bytes 24580
  3.3 14.4 %copy-start.13 = (s32[8,256]{1,0:T(8,128)S(1)}, s32[8,256]{1,0:T(8,128)}, u32[]{:S(2)}) copy-start(s32[8,256]{1,0:T(8,128)} %mask.1) | copy-start | bytes 24580
  3.3 14.4 %copy-start.14 = (f32[256]{0:T(256)S(1)}, f32[256]{0:T(256)}, u32[]{:S(2)}) copy-start(f32[256]{0:T(256)} %param.16) | copy-start | bytes 3076
  3.3 14.4 %all-to-all-start = ((f32[32,1,128]{2,1,0:T(1,128)}), f32[32,1,128]{2,1,0:T(1,128)S(1)}, u32[]{:S(2)}, u32[]{:S(2)}) async-start(f32[32,1,128]{2,1,0:T(1,128)} %bitcast.1), calls=%async_computation | async-start | bytes 32768 | tf_op jit(solution)/shard_map/all_to_all | solution.py:300
  10.6 1.1 %copy-start = (f32[6,6,4096]{2,1,0:T(8,128)S(1)}, f32[6,6,4096]{2,1,0:T(8,128)}, u32[]{:S(2)}) copy-start(f32[6,6,4096]{2,1,0:T(8,128)} %precond.3) | copy-start | bytes 1769476
  11.7 0.9 %copy-start.4 = (f32[6,4096]{1,0:T(8,128)S(1)}, f32[6,4096]{1,0:T(8,128)}, u32[]{:S(2)}) copy-start(f32[6,4096]{1,0:T(8,128)} %residual.3) | copy-start | bytes 294916
  12.6 0.9 %copy-start.6 = (f32[6,4096]{1,0:T(8,128)S(1)}, f32[6,4096]{1,0:T(8,128)}, u32[]{:S(2)}) copy-start(f32[6,4096]{1,0:T(8,128)} %damping.3) | copy-start | bytes 294916
  13.5 4.2 %copy-start.8 = (f32[2,9,8,256]{3,2,1,0:T(8,128)S(1)}, f32[2,9,8,256]{3,2,1,0:T(8,128)}, u32[]{:S(2)}) copy-start(f32[2,9,8,256]{3,2,1,0:T(8,128)} %jac.1) | copy-start | bytes 442372
  13.5 14.6 %copy-start.1 = (f32[6,6,4096]{2,1,0:T(8,128)S(1)}, f32[6,6,4096]{2,1,0:T(8,128)}, u32[]{:S(2)}) copy-start(f32[6,6,4096]{2,1,0:T(8,128)} %precond.3) | copy-start | bytes 1769476
  13.5 14.6 %copy-start.7 = (f32[6,4096]{1,0:T(8,128)S(1)}, f32[6,4096]{1,0:T(8,128)}, u32[]{:S(2)}) copy-start(f32[6,4096]{1,0:T(8,128)} %damping.3) | copy-start | bytes 294916
  13.5 14.6 %copy-start.9 = (f32[6,4096]{1,0:T(8,128)S(1)}, f32[6,4096]{1,0:T(8,128)}, u32[]{:S(2)}) copy-start(f32[6,4096]{1,0:T(8,128)} %solution.1) | copy-start | bytes 294916
  13.8 14.4 %copy-start.5 = (f32[6,4096]{1,0:T(8,128)S(1)}, f32[6,4096]{1,0:T(8,128)}, u32[]{:S(2)}) copy-start(f32[6,4096]{1,0:T(8,128)} %residual.3) | copy-start | bytes 294916
  18.5 9.6 %copy-start.11 = (s32[1,512]{1,0:T(1,128)S(1)}, s32[1,512]{1,0:T(1,128)}, u32[]{:S(2)}) copy-start(s32[1,512]{1,0:T(1,128)} %served.3) | copy-start | bytes 6148

commit v2 on v1

--- a/solution.py
+++ b/solution.py
@@ -86,26 +86,61 @@
     return total
 
 
-def serve_kernel(cap, direction, served, outgoing):
+def serve_kernel(cap, direction_far, served_far, outgoing, direction, served, table, sems):
     params, count = direction.shape
     groups = served.shape[1] // LANES
     per = LANES // cap
-
-    def body(j):
-        row = served[:, at_group(j)]
-        low = spread(row % LANES, params)
-        high = spread(row // LANES, params)
-        rows = jnp.zeros((params, LANES), jnp.float32)
-        for h in range(count // LANES):
-            picked = lane_gather(direction[:, h * LANES : (h + 1) * LANES], low)
-            rows = jnp.where(high == h, picked, rows)
-        outgoing[at_rows(j, per), :] = rows_to_blocks(rows, cap, params)
-
-    each(groups, body)
-
-
-def norms_kernel(direction, residual, damping, precond, norms):
+    cuts = sems.shape[0] - 1
+    width = count // cuts
+    head = pltpu.make_async_copy(served_far, served, sems.at[cuts])
+    head.start()
+    pieces = []
+    for c in range(cuts):
+        at = pl.ds(c * width, width)
+        pieces.append(
+            pltpu.make_async_copy(direction_far.at[:, at], direction.at[:, at], sems.at[c])
+        )
+        pieces[-1].start()
+    head.wait()
+
+    for c in range(cuts):
+        pieces[c].wait()
+
+        def body(j):
+            row = served[:, at_group(j)]
+            low = spread(row % LANES, params)
+            high = spread(row // LANES, params)
+            if c == 0:
+                rows = jnp.zeros((params, LANES), jnp.float32)
+            else:
+                rows = table[:, at_group(j)]
+            for h in range(c * width // LANES, (c + 1) * width // LANES):
+                picked = lane_gather(direction[:, h * LANES : (h + 1) * LANES], low)
+                rows = jnp.where(high == h, picked, rows)
+            if c + 1 < cuts:
+                table[:, at_group(j)] = rows
+            else:
+                outgoing[at_rows(j, per), :] = rows_to_blocks(rows, cap, params)
+
+        each(groups, body)
+
+
+def norms_kernel(
+    direction_far, residual_far, damping_far, precond_far, norms,
+    direction, residual, damping, precond, sems,
+):
     params, count = direction.shape
+    pairs = [
+        (precond_far, precond),
+        (residual_far, residual),
+        (direction_far, direction),
+        (damping_far, damping),
+    ]
+    copies = [pltpu.make_async_copy(far, near, sems.at[i]) for i, (far, near) in enumerate(pairs)]
+    for copy in copies:
+        copy.start()
+    for copy in copies:
+        copy.wait()
     old = jnp.zeros((params, LANES), jnp.float32)
     curv = jnp.zeros((params, LANES), jnp.float32)
     for h in range(count // LANES):
@@ -285,15 +320,20 @@
         direction_new[:, at] = pre_new[:, at] + ratio * direction[:, at]
 
 
-def call(kernel, outs, scratch=(), cost=0):
+def call(kernel, outs, scratch=(), cost=0, far=0):
     shapes = [jax.ShapeDtypeStruct(o, jnp.float32) for o in outs]
-    return pl.pallas_call(
+    places = {"in_specs": [pl.BlockSpec(memory_space=pltpu.HBM)] * far} if far else {}
+    run = pl.pallas_call(
         kernel,
+        **places,
         out_shape=shapes[0] if len(shapes) == 1 else shapes,
         scratch_shapes=scratch,
         compiler_params=pltpu.CompilerParams(vmem_limit_bytes=32 * 1024 * 1024),
         cost_estimate=pl.CostEstimate(flops=cost, bytes_accessed=cost, transcendentals=0),
     )
+    if not far:
+        return run
+    return lambda *args: run(*[pltpu.with_memory_space_constraint(a, pltpu.HBM) for a in args])
 
 
 def exchange(blocks):
@@ -317,9 +357,33 @@
     cap = serve_rows.shape[1] // devices
     block = (devices, LANES)
 
-    outgoing = call(functools.partial(serve_kernel, cap), [block], cost=400_000)(direction, serve_rows)
+    local = pltpu.VMEM(direction.shape, jnp.float32)
+    outgoing = call(
+        functools.partial(serve_kernel, cap),
+        [block],
+        scratch=[
+            local,
+            pltpu.VMEM(serve_rows.shape, jnp.int32),
+            pltpu.VMEM((params, serve_rows.shape[1]), jnp.float32),
+            pltpu.SemaphoreType.DMA((5,)),
+        ],
+        cost=400_000,
+        far=2,
+    )(direction, serve_rows)
     incoming = exchange(outgoing)
-    norms = call(norms_kernel, [(SUBS, LANES)], cost=2_000_000)(direction, residual, cam_damping, precond)
+    norms = call(
+        norms_kernel,
+        [(SUBS, LANES)],
+        scratch=[
+            local,
+            local,
+            local,
+            pltpu.VMEM(precond.shape, jnp.float32),
+            pltpu.SemaphoreType.DMA((4,)),
+        ],
+        cost=2_000_000,
+        far=4,
+    )(direction, residual, cam_damping, precond)
     returned = call(
         functools.partial(track_kernel, cap, params),
         [block],

time: 39.3 us -> 38 us (0.967)
  local copies, waits for them, and re-layouts: 4.56 us -> 0.06 us
  Pallas kernels: 3.99 us -> 6.46 us
  waiting for transfers between devices: 3.9 us -> 5.41 us
  blocking collectives: 18.4 us -> 17.8 us
    unnamed x30 -> x20, local copies, waits for them, and re-layouts: 4.56 us -> 0.06 us
    pallas_call x2, Pallas kernels: 1.27 us -> 3.74 us  [call(): run(*[pltpu.with_memory_space_constraint(a, pltpu.HBM) for a in args])]
    all_to_all x1, waiting for transfers between devices: 3.9 us -> 5.41 us  [exchange(): return lax.all_to_all(blocks, AXES, split_axis=0, concat_axis=0, tiled=True)]
    all_to_all x2, blocking collectives: 18.4 us -> 17.8 us  [exchange(): return lax.all_to_all(blocks, AXES, split_axis=0, concat_axis=0, tiled=True)]
  transfers between devices with their start and end apart: 1 -> 1, of which waited for: 1 -> 1; matrix products, arithmetic and copies ran while one was open for 0% -> 0% of each run, Pallas kernels for 1% -> 4%
where the time goes in v2:
time: 38 us; the launch traced here: 37.8 us
  blocking collectives  17.8 us (47%)
  starting transfers between devices  7.3 us (19%)
  Pallas kernels  6.46 us (17%)
  waiting for transfers between devices  5.41 us (14%)
  between operations  0.78 us (2%)
    all_to_all x2, blocking collectives, exchange(): return lax.all_to_all(blocks, AXES, split_axis=0, concat_axis=0, tiled=True)  17.8 us
    all_to_all x1, starting transfers between devices, exchange(): return lax.all_to_all(blocks, AXES, split_axis=0, concat_axis=0, tiled=True)  7.3 us
    all_to_all x1, waiting for transfers between devices, exchange(): return lax.all_to_all(blocks, AXES, split_axis=0, concat_axis=0, tiled=True)  5.41 us
    pallas_call x2, Pallas kernels, call(): run(*[pltpu.with_memory_space_constraint(a, pltpu.HBM) for a in args])  3.74 us
    pallas_call x1, Pallas kernels, on_device(): call(functools.partial(owner_kernel, cap), [direction.shape, direction.sh...  1.21 us
    pallas_call x1, Pallas kernels, on_device(): call(functools.partial(track_kernel, cap, params), [block], scratch=[pltp...  0.83 us
  transfers between devices with their start and end apart: 1, of which 1 were waited for; matrix products, arithmetic and copies ran while one was open for 0% of the time, Pallas kernels for 4%

profile of v2, /device:TPU:0, one launch (start us, length us, event | category | flops | bytes accessed | tf_op | source)
XLA Modules:
  0.0 37.8 jit_solution(16520986292951089952)
XLA Ops:
  0.6 0.0 copy-start
  0.6 2.1 %shard_map.121 = f32[32,128]{1,0:T(8,128)} custom-call(f32[6,4096]{1,0:T(8,128)} %direction.3, s32[1,512]{1,0:T(1,128)} %served.1), custom_call_target="tpu_custom_call" | custom-call | flops 400000 | bytes 400000 | tf_op jit(solution)/shard_map/pallas_call | solution.py:336
  2.8 7.3 %all-to-all-start = ((f32[32,1,128]{2,1,0:T(1,128)}), f32[32,1,128]{2,1,0:T(1,128)S(1)}, u32[]{:S(2)}, u32[]{:S(2)}) async-start(f32[32,1,128]{2,1,0:T(1,128)} %bitcast.1), calls=%async_computation | async-start | bytes 32768 | tf_op jit(solution)/shard_map/all_to_all | solution.py:340
  10.1 0.0 copy-start.4
  10.1 0.0 copy-start.7
  10.1 0.0 copy-start.8
  10.1 0.0 copy-start.9
  10.1 0.0 copy-start.2
  10.2 0.0 copy-start.3
  10.2 0.0 copy-start.5
  10.2 1.6 %shard_map.122.norms = f32[8,128]{1,0:T(8,128)S(1)} custom-call(f32[6,4096]{1,0:T(8,128)} %direction.3, f32[6,4096]{1,0:T(8,128)} %residual.1, f32[6,4096]{1,0:T(8,128)} %damping.1, f32[6,6,4096]{2,1,0:T(8,128)} %precond.1), custom_call_target="tpu_custom_call" | custom-call | flops 2000000 | bytes 2000000 | tf_op jit(solution)/shard_map/pallas_call | solution.py:336
  11.8 0.0 copy-start.1
  11.8 5.4 %all-to-all-done = f32[32,1,128]{2,1,0:T(1,128)S(1)} async-done(((f32[32,1,128]{2,1,0:T(1,128)}), f32[32,1,128]{2,1,0:T(1,128)S(1)}, u32[]{:S(2)}, u32[]{:S(2)}) %all-to-all-start) | async-done | bytes 16416 | tf_op jit(solution)/shard_map/all_to_all | solution.py:340
  17.2 0.0 copy-done.9
  17.2 0.8 %shard_map.123 = f32[32,128]{1,0:T(8,128)S(1)} custom-call(f32[32,128]{1,0:T(8,128)S(1)} %bitcast.13, f32[2,9,8,256]{3,2,1,0:T(8,128)S(1)} %copy-done.4, s32[8,256]{1,0:T(8,128)S(1)} %copy-done.7, s32[8,256]{1,0:T(8,128)S(1)} %copy-done.8, f32[1,256]{1,0:T(1,128)S(1)} %bitcast.18, f32[8,128]{1,0:T(8,128)S(1)} %shard_map.122.norms), custom_call_target="tpu_custom_call" | custom-call | flops 2000000 | bytes 2000000 | tf_op jit(solution)/shard_map/pallas_call | solution.py:387
  18.1 0.0 copy-start.6
  18.1 8.9 %all_to_all.33 = f32[32,1,128]{2,1,0:T(1,128)S(1)} all-to-all(f32[32,1,128]{2,1,0:T(1,128)S(1)} %bitcast.15), channel_id=1, replica_groups=mesh['track'=16,'ses'=2] {'track','ses'}, dimensions={0} | all-to-all | bytes 32768 | tf_op jit(solution)/shard_map/all_to_all | solution.py:340
  27.0 0.0 copy-done.3
  27.0 0.0 copy-done.5
  27.0 0.0 copy-done.1
  27.0 0.0 copy-done.6
  27.0 1.2 %shard_map.124 = (f32[6,4096]{1,0:T(8,128)}, f32[6,4096]{1,0:T(8,128)}, f32[6,4096]{1,0:T(8,128)S(1)}, f32[32,128]{1,0:T(8,128)S(1)}, f32[8,128]{1,0:T(8,128)S(1)}) custom-call(f32[32,128]{1,0:T(8,128)S(1)} %bitcast.16, s32[1,512]{1,0:T(1,128)S(1)} %copy-done.6, f32[6,4096]{1,0:T(8,128)S(1)} %copy-done.1, f32[6,4096]{1,0:T(8,128)S(1)} %copy-done.2, ...), custom_call_target="tpu_custom_call" | custom-call | flops 2000000 | bytes 2000000 | tf_op jit(solution)/shard_map/pallas_call | solution.py:394
  28.2 8.9 %all_to_all.34 = f32[32,1,128]{2,1,0:T(1,128)S(1)} all-to-all(f32[32,1,128]{2,1,0:T(1,128)S(1)} %bitcast.17), channel_id=1, replica_groups=mesh['track'=16,'ses'=2] {'track','ses'}, dimensions={0} | all-to-all | bytes 32768 | tf_op jit(solution)/shard_map/all_to_all | solution.py:340
  37.1 0.7 %shard_map.125 = f32[6,4096]{1,0:T(8,128)} custom-call(f32[32,128]{1,0:T(8,128)S(1)} %bitcast.14, f32[8,128]{1,0:T(8,128)S(1)} %get-tuple-element.11.old_norm, f32[6,4096]{1,0:T(8,128)S(1)} %copy-done.1, f32[6,4096]{1,0:T(8,128)S(1)} %get-tuple-element.12.pre_new), custom_call_target="tpu_custom_call" | custom-call | flops 400000 | bytes 400000 | tf_op jit(solution)/shard_map/pallas_call | solution.py:401
  (5 shorter events, 0.0 us)
Async XLA Ops:
  0.6 26.4 %copy-start = (f32[6,6,4096]{2,1,0:T(8,128)S(1)}, f32[6,6,4096]{2,1,0:T(8,128)}, u32[]{:S(2)}) copy-start(f32[6,6,4096]{2,1,0:T(8,128)} %precond.1) | copy-start | bytes 1769476
  2.8 14.4 %all-to-all-start = ((f32[32,1,128]{2,1,0:T(1,128)}), f32[32,1,128]{2,1,0:T(1,128)S(1)}, u32[]{:S(2)}, u32[]{:S(2)}) async-start(f32[32,1,128]{2,1,0:T(1,128)} %bitcast.1), calls=%async_computation | async-start | bytes 32768 | tf_op jit(solution)/shard_map/all_to_all | solution.py:340
  10.1 7.1 %copy-start.4 = (f32[2,9,8,256]{3,2,1,0:T(8,128)S(1)}, f32[2,9,8,256]{3,2,1,0:T(8,128)}, u32[]{:S(2)}) copy-start(f32[2,9,8,256]{3,2,1,0:T(8,128)} %jac.1) | copy-start | bytes 442372
  10.1 7.1 %copy-start.7 = (s32[8,256]{1,0:T(8,128)S(1)}, s32[8,256]{1,0:T(8,128)}, u32[]{:S(2)}) copy-start(s32[8,256]{1,0:T(8,128)} %slots.1) | copy-start | bytes 24580
  10.1 7.1 %copy-start.8 = (s32[8,256]{1,0:T(8,128)S(1)}, s32[8,256]{1,0:T(8,128)}, u32[]{:S(2)}) copy-start(s32[8,256]{1,0:T(8,128)} %mask.1) | copy-start | bytes 24580
  10.1 7.1 %copy-start.9 = (f32[256]{0:T(256)S(1)}, f32[256]{0:T(256)}, u32[]{:S(2)}) copy-start(f32[256]{0:T(256)} %param.16) | copy-start | bytes 3076
  10.1 16.8 %copy-start.2 = (f32[6,4096]{1,0:T(8,128)S(1)}, f32[6,4096]{1,0:T(8,128)}, u32[]{:S(2)}) copy-start(f32[6,4096]{1,0:T(8,128)} %residual.1) | copy-start | bytes 294916
  10.2 16.8 %copy-start.3 = (f32[6,4096]{1,0:T(8,128)S(1)}, f32[6,4096]{1,0:T(8,128)}, u32[]{:S(2)}) copy-start(f32[6,4096]{1,0:T(8,128)} %damping.1) | copy-start | bytes 294916
  10.2 16.8 %copy-start.5 = (f32[6,4096]{1,0:T(8,128)S(1)}, f32[6,4096]{1,0:T(8,128)}, u32[]{:S(2)}) copy-start(f32[6,4096]{1,0:T(8,128)} %solution.1) | copy-start | bytes 294916
  11.8 15.2 %copy-start.1 = (f32[6,4096]{1,0:T(8,128)S(1)}, f32[6,4096]{1,0:T(8,128)}, u32[]{:S(2)}) copy-start(f32[6,4096]{1,0:T(8,128)} %direction.3) | copy-start | bytes 294916
  18.1 8.9 %copy-start.6 = (s32[1,512]{1,0:T(1,128)S(1)}, s32[1,512]{1,0:T(1,128)}, u32[]{:S(2)}) copy-start(s32[1,512]{1,0:T(1,128)} %served.1) | copy-start | bytes 6148

commit v3 on v1

v3 whole, which is shorter than its diff:
```python
import functools

import jax
import jax.numpy as jnp
from jax import lax
from jax.experimental import pallas as pl
from jax.experimental.pallas import tpu as pltpu
from jax.sharding import PartitionSpec as P

LANES = 128
SUBS = 8
WIDE = 256
AXES = ("track", "ses")


def lane_gather(rows, index):
    return jnp.take_along_axis(rows, index, axis=1, mode="promise_in_bounds")


def spread(row, subs=SUBS):
    return jnp.broadcast_to(row, (subs, row.shape[1]))


def part(value, size):
    return value >> (size.bit_length() - 1) if size & (size - 1) == 0 else lax.div(value, jnp.int32(size))


def rest(value, size):
    return value & (size - 1) if size & (size - 1) == 0 else lax.rem(value, jnp.int32(size))


def iota(shape, dim):
    return lax.broadcasted_iota(jnp.int32, shape, dim)


def each(count, body):
    if count <= 8:
        for j in range(count):
            body(j)
    else:
        lax.fori_loop(0, count, lambda j, c: (body(j), c)[1], 0)


def at_group(j):
    if isinstance(j, int):
        return pl.ds(j * LANES, LANES)
    return pl.ds(pl.multiple_of(j * LANES, LANES), LANES)


def at_rows(j, size=SUBS):
    if isinstance(j, int):
        return pl.ds(j * size, size)
    return pl.ds(pl.multiple_of(j * size, size), size)


def rows_to_blocks(rows, cap, params):
    per = LANES // cap
    lane = iota((per, LANES), 1)
    index = iota((per, LANES), 0) * cap + rest(lane, cap)
    out = jnp.zeros((per, LANES), rows.dtype)
    for k in range(params):
        picked = lane_gather(spread(rows[k : k + 1], per), index)
        out = jnp.where(part(lane, cap) == k, picked, out)
    return out


def blocks_to_rows(blocks, cap, params):
    per = LANES // cap
    lane = iota((SUBS, LANES), 1)
    sub = iota((SUBS, LANES), 0)
    index = jnp.minimum(sub, params - 1) * cap + rest(lane, cap)
    out = jnp.zeros((SUBS, LANES), blocks.dtype)
    for src in range(per):
        picked = lane_gather(spread(blocks[src : src + 1]), index)
        out = jnp.where(part(lane, cap) == src, picked, out)
    return jnp.where(sub < params, out, 0.0)


def split_bf16(value, parts):
    pieces = []
    rest = value
    for p in range(parts):
        piece = rest.astype(jnp.bfloat16)
        pieces.append(piece)
        if p + 1 < parts:
            rest = rest - piece.astype(jnp.float32)
    return pieces


def split_rounded(value, parts):
    return [piece.astype(jnp.float32) for piece in split_bf16(value, parts)]


def apply_precond(precond, vector):
    params = vector.shape[0]
    total = precond[0] * vector[0:1]
    for k in range(1, params):
        total = total + precond[k] * vector[k : k + 1]
    return total


def one_hot(row, width):
    rows = iota((width, row.shape[1]), 0) == spread(row, width)
    return jnp.where(rows, 1.0, 0.0).astype(jnp.bfloat16)


def norms_of(direction, residual, damping, precond):
    params, count = residual.shape
    old = jnp.zeros((params, LANES), jnp.float32)
    curv = jnp.zeros((params, LANES), jnp.float32)
    for h in range(count // LANES):
        at = slice(h * LANES, (h + 1) * LANES)
        res = residual[:, at]
        pre = apply_precond([precond[k, :, at] for k in range(params)], res)
        old = old + res * pre
        dire = direction[0:params, at]
        curv = curv + damping[:, at] * dire * dire
    return jnp.sum(old), jnp.sum(curv)


def serve_kernel(direction_far, served_far, damp_far, rows, direction, served, damp, padded, sems):
    params, count = direction_far.shape
    slab = min(served.shape[1], 4 * LANES)
    highs = count // WIDE
    copies = [
        pltpu.make_async_copy(direction_far, direction, sems.at[0]),
        pltpu.make_async_copy(served_far, served, sems.at[1]),
        pltpu.make_async_copy(damp_far, damp, sems.at[2]),
    ]
    for copy in copies:
        copy.start()
    padded[params:SUBS, :] = jnp.zeros((SUBS - params, count), jnp.float32)
    copies[1].wait()
    one_slab = slab == served.shape[1]

    def places(j):
        row = served[:, at_rows(j, slab)]
        return one_hot(rest(row, WIDE), WIDE), spread(part(row, WIDE))

    first = places(0) if one_slab else None
    copies[2].wait()
    copies[0].wait()
    padded[0:params, :] = direction[...]
    stacked = jnp.concatenate([padded[:, h * WIDE : (h + 1) * WIDE] for h in range(highs)], axis=0)
    stacked = jnp.concatenate(split_bf16(stacked, 3), axis=0)

    def serve(j):
        at_low, high = first if one_slab else places(j)
        found = jnp.dot(stacked, at_low, preferred_element_type=jnp.float32)
        found = found.reshape(3, highs, SUBS, slab)
        pieces = [found[p, 0] for p in range(3)]
        for h in range(1, highs):
            here = high == h
            pieces = [jnp.where(here, found[p, h], pieces[p]) for p in range(3)]
        rows[:, at_rows(j, slab)] = pieces[0] + pieces[1] + pieces[2]

    each(served.shape[1] // slab, serve)


def arrange_kernel(cap, params, rows, outgoing):
    per = LANES // cap

    def body(j):
        outgoing[at_rows(j, per), :] = rows_to_blocks(rows[:, at_group(j)], cap, params)

    each(rows.shape[1] // LANES, body)


def track_kernel(
    cap, params, incoming, jac, slots, mask, damp, direction, residual, damping, precond,
    returned, table,
):
    devices = incoming.shape[0]
    per = LANES // cap
    groups = devices // per
    obs, tracks = slots.shape

    def fill(j):
        table[:, at_group(j)] = blocks_to_rows(incoming[at_rows(j, per), :], cap, params)

    each(groups, fill)

    slot = slots[...]
    owner = part(slot, cap)
    within = rest(slot, cap)
    halves = [slice(t * LANES, (t + 1) * LANES) for t in range(tracks // LANES)]
    low = [rest(slot[:, at], LANES) for at in halves]
    high = [part(slot[:, at], LANES) for at in halves]

    def look(j, camera):
        rows = table[:, at_group(j)]
        out = []
        for k in range(params):
            source = spread(rows[k : k + 1], obs)
            for t in range(len(halves)):
                picked = lane_gather(source, low[t])
                out.append(jnp.where(high[t] == j, picked, camera[len(out)]))
        return tuple(out)

    camera = tuple(jnp.zeros((obs, LANES), jnp.float32) for _ in range(params * len(halves)))
    if groups <= 8:
        for j in range(groups):
            camera = look(j, camera)
    else:
        camera = lax.fori_loop(0, groups, look, camera)
    camera = [
        jnp.concatenate(camera[k * len(halves) : (k + 1) * len(halves)], axis=1)
        for k in range(params)
    ]

    live = mask[...].astype(jnp.float32)
    cam = [[jac[a, k] for k in range(params)] for a in range(2)]
    land = [[jac[a, params + i] for i in range(3)] for a in range(2)]
    projected = []
    for a in range(2):
        total = cam[a][0] * camera[0]
        for k in range(1, params):
            total = total + cam[a][k] * camera[k]
        projected.append(total)
    weighted = [[land[a][i] * live for i in range(3)] for a in range(2)]

    def over_slots(value):
        return jnp.sum(value, axis=0, keepdims=True)

    normal = {}
    for i in range(3):
        for j in range(i, 3):
            entry = over_slots(weighted[0][i] * land[0][j] + weighted[1][i] * land[1][j])
            if i == j:
                entry = entry + damp[...]
            normal[i, j] = entry
            normal[j, i] = entry
    rhs = [over_slots(weighted[0][i] * projected[0] + weighted[1][i] * projected[1]) for i in range(3)]
    cof = [
        [
            normal[(i + 1) % 3, (j + 1) % 3] * normal[(i + 2) % 3, (j + 2) % 3]
            - normal[(i + 1) % 3, (j + 2) % 3] * normal[(i + 2) % 3, (j + 1) % 3]
            for j in range(3)
        ]
        for i in range(3)
    ]
    det = normal[0, 0] * cof[0][0] + normal[0, 1] * cof[0][1] + normal[0, 2] * cof[0][2]
    step = [
        (cof[0][i] * rhs[0] + cof[1][i] * rhs[1] + cof[2][i] * rhs[2]) / det for i in range(3)
    ]
    res = [
        live
        * (projected[a] - (land[a][0] * step[0] + land[a][1] * step[1] + land[a][2] * step[2]))
        for a in range(2)
    ]
    curv = jnp.sum(res[0] * projected[0] + res[1] * projected[1])
    grad = [cam[0][k] * res[0] + cam[1][k] * res[1] for k in range(params)]

    owner_id = iota((devices, tracks), 0)
    within_id = iota((cap, tracks), 0)
    pieces = [split_rounded(grad[k], 2) for k in range(params)]
    owners, values = [], []
    for o in range(obs):
        at_owner = spread(owner[o : o + 1], devices) == owner_id
        owners.append(jnp.where(at_owner, 1.0, 0.0).astype(jnp.bfloat16))
        at_within = spread(within[o : o + 1], cap) == within_id
        values.append(
            [
                jnp.concatenate(
                    [
                        jnp.where(at_within, spread(pieces[k][p][o : o + 1], cap), 0.0)
                        for k in range(params)
                    ],
                    axis=0,
                ).astype(jnp.bfloat16)
                for p in range(2)
            ]
        )
    total = lax.dot_general(
        jnp.concatenate(owners * 2, axis=1),
        jnp.concatenate([values[o][p] for p in range(2) for o in range(obs)], axis=1),
        (((1,), (1,)), ((), ())),
        preferred_element_type=jnp.float32,
    )
    used = params * cap
    spare = (devices, LANES - used)
    old, own_curv = norms_of(direction, residual, damping, precond)
    returned[:, 0:used] = total
    returned[:, used:LANES] = jnp.where(iota(spare, 1) == 0, old, own_curv + curv)


def owner_kernel(
    cap, arrived, served, direction, residual, solution, damping, precond,
    solution_new, residual_new, pre_new, norm_block, old_norm, summed,
):
    params, count = residual.shape
    devices = arrived.shape[0]
    per = LANES // cap
    slab = min(devices // per, 4)
    highs = count // LANES
    wide_highs = count // WIDE

    def body(j, first):
        weights, lows = [[], []], []
        for g in range(slab):
            rows = blocks_to_rows(arrived[at_rows(j * slab + g, per), :], cap, params)
            row = served[:, at_group(j * slab + g)]
            lows.append(one_hot(rest(row, WIDE), WIDE))
            high = spread(part(row, WIDE))
            for p, piece in enumerate(split_rounded(rows, 2)):
                weights[p].append(
                    jnp.concatenate(
                        [jnp.where(high == h, piece, 0.0) for h in range(wide_highs)], axis=0
                    ).astype(jnp.bfloat16)
                )
        total = lax.dot_general(
            jnp.concatenate([jnp.concatenate(weights[p], axis=1) for p in range(2)], axis=0),
            jnp.concatenate(lows, axis=1),
            (((1,), (1,)), ((), ())),
            preferred_element_type=jnp.float32,
        )
        total = total[: wide_highs * SUBS] + total[wide_highs * SUBS :]
        summed[...] = total if first else summed[...] + total

    slabs = devices // per // slab
    body(0, True)
    if slabs > 1:
        lax.fori_loop(1, slabs, lambda j, c: (body(j, False), c)[1], 0)

    totals = jnp.sum(arrived[...], axis=0, keepdims=True)
    old = totals[:, params * cap : params * cap + 1]
    curv = totals[:, params * cap + 1 : params * cap + 2]
    step_size = old / curv
    step = jnp.broadcast_to(step_size, (params, LANES))
    new = jnp.zeros((params, LANES), jnp.float32)
    for h in range(highs):
        at = slice(h * LANES, (h + 1) * LANES)
        dire = direction[0:params, at]
        image = damping[:, at] * dire + summed[h // 2 * SUBS : h // 2 * SUBS + params, h % 2 * LANES : (h % 2 + 1) * LANES]
        solution_new[:, at] = solution[:, at] + step * dire
        res = residual[:, at] - step * image
        residual_new[:, at] = res
        pre = apply_precond([precond[k, :, at] for k in range(params)], res)
        pre_new[:, at] = pre
        new = new + res * pre
    norm_block[...] = jnp.broadcast_to(jnp.sum(new), norm_block.shape)
    old_norm[...] = jnp.broadcast_to(old, old_norm.shape)


def final_kernel(
    norm_blocks, old_norm, direction, pre_new, solution_near, residual_near,
    solution_new, residual_new, direction_new, local, sems,
):
    params, count = pre_new.shape
    cuts = sems.shape[0] - 2
    width = count // cuts
    copies = [
        pltpu.make_async_copy(solution_near, solution_new, sems.at[cuts]),
        pltpu.make_async_copy(residual_near, residual_new, sems.at[cuts + 1]),
    ]
    for copy in copies:
        copy.start()
    new = jnp.sum(norm_blocks[...], axis=0, keepdims=True)
    ratio = jnp.broadcast_to(new / old_norm[0:1, :], (params, LANES))
    for c in range(cuts):
        for h in range(c * width // LANES, (c + 1) * width // LANES):
            at = slice(h * LANES, (h + 1) * LANES)
            local[:, at] = pre_new[:, at] + ratio * direction[0:params, at]
        at = pl.ds(c * width, width)
        copies.append(pltpu.make_async_copy(local.at[:, at], direction_new.at[:, at], sems.at[c]))
        copies[-1].start()
    for copy in copies:
        copy.wait()


def call(kernel, outs, scratch=(), cost=0, far=0, near=(), out=None):
    outs = [o if hasattr(o, "dtype") else jax.ShapeDtypeStruct(o, jnp.float32) for o in outs]
    shapes = [
        pltpu.VMEM(o.shape, o.dtype) if i in near else jax.ShapeDtypeStruct(o.shape, o.dtype)
        for i, o in enumerate(outs)
    ]
    away = pl.BlockSpec(memory_space=pltpu.HBM)
    places = {"in_specs": [away] * far} if far else {}
    if out == "far":
        places["out_specs"] = [away] * len(outs)
    run = pl.pallas_call(
        kernel,
        **places,
        out_shape=shapes[0] if len(shapes) == 1 else shapes,
        scratch_shapes=scratch,
        compiler_params=pltpu.CompilerParams(vmem_limit_bytes=32 * 1024 * 1024),
        cost_estimate=pl.CostEstimate(flops=cost, bytes_accessed=cost, transcendentals=0),
    )
    if not far:
        return run
    return lambda *args: run(*[pltpu.with_memory_space_constraint(a, pltpu.HBM) for a in args])


def exchange(blocks):
    return lax.all_to_all(blocks, AXES, split_axis=0, concat_axis=0, tiled=True)


def on_device(
    jacobians,
    direction,
    residual,
    solution,
    cam_damping,
    precond,
    land_damping,
    obs_slot,
    obs_mask,
    serve_rows,
):
    devices = lax.axis_size("track") * lax.axis_size("ses")
    params = direction.shape[0]
    cap = serve_rows.shape[1] // devices
    block = (devices, LANES)

    damp = land_damping.reshape(1, -1)
    rows, near_direction, near_served, near_damp = call(
        serve_kernel,
        [(SUBS, devices * cap), direction, serve_rows, damp],
        scratch=[
            pltpu.VMEM((SUBS, direction.shape[1]), jnp.float32),
            pltpu.SemaphoreType.DMA((3,)),
        ],
        cost=20_000,
        far=3,
        near=(0, 1, 2, 3),
    )(direction, serve_rows, damp)
    outgoing = call(
        functools.partial(arrange_kernel, cap, params), [block], cost=2_000_000_000, near=(0,)
    )(rows)
    incoming = exchange(outgoing)
    returned = call(
        functools.partial(track_kernel, cap, params),
        [block],
        scratch=[pltpu.VMEM((SUBS, devices * cap), jnp.float32)],
        cost=2_000_000,
    )(
        incoming, jacobians, obs_slot, obs_mask, near_damp,
        near_direction, residual, cam_damping, precond,
    )
    arrived = exchange(returned)
    solution_new, residual_new, pre_new, norm_block, old_norm = call(
        functools.partial(owner_kernel, cap),
        [direction.shape, direction.shape, direction.shape, block, (SUBS, LANES)],
        scratch=[pltpu.VMEM((direction.shape[1] // WIDE * SUBS, WIDE), jnp.float32)],
        cost=2_000_000,
        near=(0, 1, 2),
    )(
        arrived, near_served, near_direction, residual, solution, cam_damping, precond
    )
    norm_blocks = exchange(norm_block)
    return tuple(
        call(
            final_kernel,
            [direction.shape] * 3,
            scratch=[pltpu.VMEM(direction.shape, jnp.float32), pltpu.SemaphoreType.DMA((4,))],
            cost=400_000,
            out="far",
        )(norm_blocks, old_norm, near_direction, pre_new, solution_new, residual_new)
    )


def solution(mesh):
    return jax.shard_map(
        on_device,
        mesh=mesh,
        in_specs=(
            P(None, None, None, AXES),
            P(None, AXES),
            P(None, AXES),
            P(None, AXES),
            P(None, AXES),
            P(None, None, AXES),
            P(AXES),
            P(None, AXES),
            P(None, AXES),
            P(AXES, None),
        ),
        out_specs=(P(None, AXES), P(None, AXES), P(None, AXES)),
        check_vma=False,
    )
```

time: 39.3 us -> 36.4 us (0.926)
  blocking collectives: 18.4 us -> 32.1 us
  starting transfers between devices: 7.3 us -> 0 us
  local copies, waits for them, and re-layouts: 4.56 us -> 0.04 us
  waiting for transfers between devices: 3.9 us -> 0 us
  Pallas kernels: 3.99 us -> 3.24 us
    all_to_all x2 -> x3, blocking collectives: 18.4 us -> 32.1 us  [exchange(): return lax.all_to_all(blocks, AXES, split_axis=0, concat_axis=0, tiled=True)]
    all_to_all x1 -> x0, starting transfers between devices: 7.3 us -> none  [exchange(): return lax.all_to_all(blocks, AXES, split_axis=0, concat_axis=0, tiled=True)]
    unnamed x30 -> x14, local copies, waits for them, and re-layouts: 4.56 us -> 0.04 us
    all_to_all x1 -> x0, waiting for transfers between devices: 3.9 us -> none  [exchange(): return lax.all_to_all(blocks, AXES, split_axis=0, concat_axis=0, tiled=True)]
    pallas_call x1, Pallas kernels: 1.21 us -> 0.52 us  [on_device(): call(functools.partial(owner_kernel, cap), [direction.shape, direction.sh...]
  transfers between devices with their start and end apart: 1 -> 0, of which waited for: 1 -> 0; matrix products, arithmetic and copies ran while one was open for 0% -> 0% of each run, Pallas kernels for 1% -> 0%
where the time goes in v3:
time: 36.4 us; the launch traced here: 36.1 us
  blocking collectives  32.1 us (88%)
  Pallas kernels  3.24 us (9%)
  between operations  0.75 us (2%)
    all_to_all x3, blocking collectives, exchange(): return lax.all_to_all(blocks, AXES, split_axis=0, concat_axis=0, tiled=True)  32.1 us
    pallas_call x1, Pallas kernels, call(): run(*[pltpu.with_memory_space_constraint(a, pltpu.HBM) for a in args])  1.19 us
    pallas_call x1, Pallas kernels, on_device(): call(final_kernel, [direction.shape] * 3, scratch=[pltpu.VMEM(direction.s...  0.77 us

profile of v3, /device:TPU:0, one launch (start us, length us, event | category | flops | bytes accessed | tf_op | source)
XLA Modules:
  0.0 36.1 jit_solution(17171015448148498204)
XLA Ops:
  0.6 1.2 %shard_map.121 = (f32[8,512]{1,0:T(8,128)S(1)}, f32[6,4096]{1,0:T(8,128)S(1)}, s32[1,512]{1,0:T(1,128)S(1)}, f32[1,256]{1,0:T(1,128)S(1)}) custom-call(f32[6,4096]{1,0:T(8,128)} %direction_far.1, s32[1,512]{1,0:T(1,128)} %served_far.1, f32[1,256]{1,0:T(1,128)} %bitcast.19), custom_call_target="tpu_custom_call" | custom-call | flops 20000 | bytes 20000 | tf_op jit(solution)/shard_map/pallas_call | solution.py:391
  1.8 0.0 copy-start
  1.8 0.0 copy-start.1
  1.9 0.0 copy-start.2
  1.9 0.0 copy-start.3
  1.9 0.1 shard_map.122
  2.0 0.0 copy-start.5
  2.0 0.0 copy-start.6
  2.0 14.3 %all_to_all.33 = f32[32,1,128]{2,1,0:T(1,128)S(1)} all-to-all(f32[32,1,128]{2,1,0:T(1,128)S(1)} %bitcast.18), channel_id=1, replica_groups=mesh['track'=16,'ses'=2] {'track','ses'}, dimensions={0} | all-to-all | bytes 32768 | tf_op jit(solution)/shard_map/all_to_all | solution.py:395
  16.3 0.0 copy-done
  16.3 0.0 copy-done.1
  16.3 0.0 copy-done.2
  16.3 0.0 copy-done.3
  16.3 0.0 copy-done.5
  16.3 0.0 copy-done.6
  16.3 0.0 copy-start.4
  16.4 0.7 %shard_map.123 = f32[32,128]{1,0:T(8,128)S(1)} custom-call(f32[32,128]{1,0:T(8,128)S(1)} %bitcast.13, f32[2,9,8,256]{3,2,1,0:T(8,128)S(1)} %copy-done.3, s32[8,256]{1,0:T(8,128)S(1)} %copy-done.5, s32[8,256]{1,0:T(8,128)S(1)} %copy-done.6, f32[1,256]{1,0:T(1,128)S(1)} %get-tuple-element.13.damp, f32[6,4096]{1,0:T(8,128)S(1)} %get-tuple-element.14.direction, ...), custom_call_target="tpu_custom_call" | custom-call | flops 2000000 | bytes 2000000 | tf_op jit(solution)/shard_map/pallas_call | solution.py:431
  17.0 8.9 %all_to_all.34 = f32[32,1,128]{2,1,0:T(1,128)S(1)} all-to-all(f32[32,1,128]{2,1,0:T(1,128)S(1)} %bitcast.14), channel_id=1, replica_groups=mesh['track'=16,'ses'=2] {'track','ses'}, dimensions={0} | all-to-all | bytes 32768 | tf_op jit(solution)/shard_map/all_to_all | solution.py:395
  25.9 0.0 copy-done.4
  25.9 0.5 %shard_map.124 = (f32[6,4096]{1,0:T(8,128)S(1)}, f32[6,4096]{1,0:T(8,128)S(1)}, f32[6,4096]{1,0:T(8,128)S(1)}, f32[32,128]{1,0:T(8,128)S(1)}, f32[8,128]{1,0:T(8,128)S(1)}) custom-call(f32[32,128]{1,0:T(8,128)S(1)} %bitcast.16, s32[1,512]{1,0:T(1,128)S(1)} %get-tuple-element.15.served, f32[6,4096]{1,0:T(8,128)S(1)} %get-tuple-element.14.direction, ...), custom_call_target="tpu_custom_call" | custom-call | flops 2000000 | bytes 2000000 | tf_op jit(solution)/shard_map/pallas_call | solution.py:441
  26.5 8.9 %all_to_all.35 = f32[32,1,128]{2,1,0:T(1,128)S(1)} all-to-all(f32[32,1,128]{2,1,0:T(1,128)S(1)} %bitcast.17), channel_id=1, replica_groups=mesh['track'=16,'ses'=2] {'track','ses'}, dimensions={0} | all-to-all | bytes 32768 | tf_op jit(solution)/shard_map/all_to_all | solution.py:395
  35.4 0.8 %shard_map.125 = (f32[6,4096]{1,0:T(8,128)}, f32[6,4096]{1,0:T(8,128)}, f32[6,4096]{1,0:T(8,128)}) custom-call(f32[32,128]{1,0:T(8,128)S(1)} %bitcast.15, f32[8,128]{1,0:T(8,128)S(1)} %get-tuple-element.17.old_norm, f32[6,4096]{1,0:T(8,128)S(1)} %get-tuple-element.14.direction, f32[6,4096]{1,0:T(8,128)S(1)} %get-tuple-element.18.pre_new, ...), custom_call_target="tpu_custom_call" | custom-call | flops 400000 | bytes 400000 | tf_op jit(solution)/shard_map/pallas_call | solution.py:452
Async XLA Ops:
  1.8 14.5 %copy-start = (f32[6,6,4096]{2,1,0:T(8,128)S(1)}, f32[6,6,4096]{2,1,0:T(8,128)}, u32[]{:S(2)}) copy-start(f32[6,6,4096]{2,1,0:T(8,128)} %precond.3) | copy-start | bytes 1769476
  1.8 14.5 %copy-start.1 = (f32[6,4096]{1,0:T(8,128)S(1)}, f32[6,4096]{1,0:T(8,128)}, u32[]{:S(2)}) copy-start(f32[6,4096]{1,0:T(8,128)} %residual.3) | copy-start | bytes 294916
  1.9 14.5 %copy-start.2 = (f32[6,4096]{1,0:T(8,128)S(1)}, f32[6,4096]{1,0:T(8,128)}, u32[]{:S(2)}) copy-start(f32[6,4096]{1,0:T(8,128)} %damping.3) | copy-start | bytes 294916
  1.9 14.5 %copy-start.3 = (f32[2,9,8,256]{3,2,1,0:T(8,128)S(1)}, f32[2,9,8,256]{3,2,1,0:T(8,128)}, u32[]{:S(2)}) copy-start(f32[2,9,8,256]{3,2,1,0:T(8,128)} %jac.1) | copy-start | bytes 442372
  2.0 14.4 %copy-start.5 = (s32[8,256]{1,0:T(8,128)S(1)}, s32[8,256]{1,0:T(8,128)}, u32[]{:S(2)}) copy-start(s32[8,256]{1,0:T(8,128)} %slots.1) | copy-start | bytes 24580
  2.0 14.4 %copy-start.6 = (s32[8,256]{1,0:T(8,128)S(1)}, s32[8,256]{1,0:T(8,128)}, u32[]{:S(2)}) copy-start(s32[8,256]{1,0:T(8,128)} %mask.1) | copy-start | bytes 24580
  16.3 9.6 %copy-start.4 = (f32[6,4096]{1,0:T(8,128)S(1)}, f32[6,4096]{1,0:T(8,128)}, u32[]{:S(2)}) copy-start(f32[6,4096]{1,0:T(8,128)} %solution.1) | copy-start | bytes 294916
